TPU v7x, 32 devices: a whole 2x2x4 slice. The times are simulated.
32 devices in a mesh: group: 2 (over y), expert: 4 (over z), tensor: 4 (over x, core).
Axes of the slice: x: 2, y: 2, z: 4, core: 2. Of those that a mesh axis runs over, the one named last changes fastest.
Arguments:
- tokens: bfloat16 [512, 4096], P(('group', 'expert'), 'tensor'), parts along dimension 0, may hold values from -400 to 400
- norm_gain: float32 [4096], replicated, may hold values from 0.1 to 1.9
- expert_ids: int32 [512, 8], P(('group', 'expert')), parts along dimension 0, may hold values from 0 to 63, all different within a row; in each aligned block of 64 rows (0 to 63, 64 to 127, ...) at most 16 rows name the same one
- gate_weights: float32 [512, 8], P(('group', 'expert')), parts along dimension 0, may hold values from 0.1 to 1
- gate_proj: bfloat16 [64, 768, 4096], P('expert', 'tensor'), may hold values from -0.09375 to 0.09375
- up_proj: bfloat16 [64, 768, 4096], P('expert', 'tensor'), may hold values from -0.09375 to 0.09375
- down_proj: bfloat16 [64, 4096, 768], P('expert', 'tensor'), may hold values from -0.21875 to 0.21875
Outputs:
- moe_out: bfloat16 [512, 4096], P(('group', 'expert'), 'tensor'), parts along dimension 0
There are 2 independent parts, one for each index of `group`. A program takes and returns all parts, laid end to end along the dimension named above; an argument that names none is the same for every part. Nothing has to cross between parts.
Inputs may be any that keep to these rules, and one draw needn't show every extreme that they name: `expert_ids`: each row names 8 different experts. Within the rows of one device (aligned blocks of 64 rows) no expert is named by more than 16 rows, a bound that some block reaches.
All inputs are finite; a program needn't handle non-finite values.
Results may differ from a plain program's by a relative error of at most 0.008.
Values may be sent and summed in bfloat16 or wider, within the bound.
A program may use at most 128 MiB of HBM per device.

v0:
```python
import jax
import jax.numpy as jnp
from jax import lax
from jax.sharding import PartitionSpec as P

D = 4096
EXPERTS = 64
TOP = 8
CAP = 16


epsilon = 1e-06


def slot_places(expert_ids):
    flat_ids = expert_ids.reshape(-1)
    onehot = (flat_ids[:, None] == jnp.arange(EXPERTS, dtype=jnp.int32)[None, :]).astype(jnp.int32)
    before = jnp.cumsum(onehot, axis=0) - onehot
    inside = jnp.sum(onehot * before, axis=1)
    return flat_ids * CAP + inside


def expert_block(slot_rows, gate_proj, up_proj, down_proj):
    sources = slot_rows.shape[0]
    local_experts = slot_rows.shape[1]
    item_count = slot_rows.shape[2]
    gate_act = jnp.einsum(
        "slcd,lfd->lfsc", slot_rows, gate_proj, preferred_element_type=jnp.float32
    )
    up_act = jnp.einsum("slcd,lfd->lfsc", slot_rows, up_proj, preferred_element_type=jnp.float32)
    hidden = (jax.nn.silu(gate_act) * up_act).astype(jnp.bfloat16)
    hidden = hidden.reshape(local_experts, hidden.shape[1], sources * item_count)
    hidden_all = lax.all_gather(hidden, "tensor", axis=1, tiled=True)
    hidden_all = hidden_all.reshape(local_experts, hidden_all.shape[1], sources, item_count)
    result = jnp.einsum(
        "lfsc,ldf->slcd", hidden_all, down_proj, preferred_element_type=jnp.float32
    ).astype(jnp.bfloat16)
    return lax.all_to_all(result, "expert", split_axis=0, concat_axis=0, tiled=True)


def body(tokens, norm_gain, expert_ids, gate_weights, gate_proj, up_proj, down_proj):
    local_experts = gate_proj.shape[0]
    groups = lax.axis_size("expert")
    tok_rows = tokens.shape[0]
    places = slot_places(expert_ids)
    owners = (
        jnp.full((EXPERTS * CAP,), tok_rows, jnp.int32)
        .at[places]
        .set(jnp.arange(places.shape[0], dtype=jnp.int32) // TOP)
    )
    values = tokens.astype(jnp.float32)
    squares = lax.psum(jnp.sum(values * values, axis=1), "tensor")
    inv_scale = lax.rsqrt(squares / D + epsilon)[:, None]
    quarter_width = tokens.shape[1]
    gain_part = lax.dynamic_slice_in_dim(
        norm_gain, lax.axis_index("tensor") * quarter_width, quarter_width
    )
    normed = (values * inv_scale * gain_part).astype(jnp.bfloat16)
    padded = jnp.concatenate([normed, jnp.zeros((1, quarter_width), jnp.bfloat16)], axis=0)
    dispatched = padded[owners].reshape(groups, local_experts, CAP, quarter_width)
    full_rows = lax.all_gather(
        lax.all_to_all(dispatched, "expert", split_axis=0, concat_axis=0, tiled=True),
        "tensor",
        axis=3,
        tiled=True,
    )
    returned = expert_block(full_rows, gate_proj, up_proj, down_proj)
    out_width = returned.shape[-1]
    flat_back = returned.reshape(EXPERTS * CAP, out_width)
    picked = flat_back[places].reshape(tok_rows, TOP, out_width).astype(jnp.float32)
    return jnp.einsum("tkd,tk->td", picked, gate_weights).astype(jnp.bfloat16)


def solution(mesh):
    return jax.shard_map(
        body,
        mesh=mesh,
        in_specs=(
            P(("group", "expert"), "tensor"),
            P(),
            P(("group", "expert"), None),
            P(("group", "expert"), None),
            P("expert", "tensor", None),
            P("expert", "tensor", None),
            P("expert", "tensor", None),
        ),
        out_specs=P(("group", "expert"), "tensor"),
        check_vma=False,
    )
```

profile of v0, /device:TPU:0, one launch (start us, length us, event | category | flops | bytes accessed | tf_op | source)
XLA Modules:
  0.0 281.1 jit_solution(12578102919068015323)
XLA Ops:
  6.5 0.8 copy.15
  7.3 0.1 eq.29
  7.4 0.1 eq.25
  7.5 0.7 broadcast_multiply_fusion
  8.2 1.2 reduce-window.6
  9.4 0.2 slice_reduce_fusion
  9.7 0.1 copy.14
  9.8 0.1 mul.56
  9.9 0.1 fusion.27
  10.0 2.4 scatter_custom_fusion
  12.5 1.0 fusion.22
  13.5 8.3 %psum.7 = f32[64]{0:T(128)S(1)} all-reduce(f32[64]{0:T(128)S(1)} %fusion.22), channel_id=1, replica_groups=mesh['group'=2,'expert'=4,'tensor'=4] {'tensor'}, use_global_device_ids=true, to_apply=%region_1.2 | all-reduce | flops 64 | bytes 512 | tf_op jit(solution)/shard_map/psum | solution.py:52
  21.9 0.7 dynamic_slice.3
  22.6 1.0 fusion.24
  23.6 4.1 %gather_fusion = bf16[1024,1024]{1,0:T(8,128)(2,1)S(1)} fusion(bf16[65,1024]{1,0:T(8,128)(2,1)S(1)} %concatenate.3, s32[1024]{0:T(1024)S(1)} %fusion.29), kind=kCustom, calls=%fused_computation | custom fusion | bytes 4198400 | tf_op jit(solution)/shard_map/gather | solution.py:60
  27.6 51.7 %all_to_all.10 = bf16[4,16,16,1024]{3,2,1,0:T(8,128)(2,1)S(1)} all-to-all(bf16[4,16,16,1024]{3,2,1,0:T(8,128)(2,1)S(1)} %bitcast.72), channel_id=1, replica_groups=mesh['group'=2,'expert'=4,'tensor'=4] {'expert'}, dimensions={0} | all-to-all | bytes 4194304 | tf_op jit(solution)/shard_map/all_to_all | solution.py:62
  79.3 1.6 copy.18
  80.9 0.2 all-gather.5.cloned.1.call-start
  81.1 57.4 %all-gather.3.cloned.1.call-done = bf16[4,16,16,4096]{3,2,0,1:T(8,128)(2,1)} async-done(((bf16[4,16,16,1024]{3,2,0,1:T(8,128)(2,1)}), bf16[4,16,16,4096]{3,2,0,1:T(8,128)(2,1)}) %all-gather.3.cloned.1.call-update) | async-done | bytes 8388624 | tf_op jit(solution)/shard_map/all_gather | solution.py:61
  138.5 14.8 %fusion.8 = f32[16,192,4,16]{1,3,2,0:T(8,128)S(1)} fusion(bf16[4,16,16,4096]{3,2,0,1:T(8,128)(2,1)} %all-gather.3.cloned.1.call-done, bf16[16,192,4096]{2,1,0:T(8,128)(2,1)} %param.11), kind=kOutput, calls=%fused_computation.10 | convolution fusion | flops 1610612736 | bytes 34340864 | tf_op jit(solution)/shard_map/slcd,lfd->lfsc/dot_general | solution.py:27
  153.3 15.0 %fusion.17 = bf16[16,192,4,16]{1,3,2,0:T(8,128)(2,1)S(1)} fusion(bf16[4,16,16,4096]{3,2,0,1:T(8,128)(2,1)} %all-gather.3.cloned.1.call-done, bf16[16,192,4096]{2,1,0:T(8,128)(2,1)} %param.12, f32[16,192,4,16]{1,3,2,0:T(8,128)S(1)} %fusion.8), kind=kOutput, calls=%fused_computation.13 | convolution fusion | flops 1611792384 | bytes 34734080 | tf_op jit(solution)/shard_map/slcd,lfd->lfsc/dot_general | solution.py:30
  168.3 1.5 copy.19
  169.8 28.7 %all-gather.5.cloned.1.call-done = bf16[16,768,64]{2,0,1:T(8,128)(2,1)} async-done(((bf16[16,192,64]{2,0,1:T(8,128)(2,1)}), bf16[16,768,64]{2,0,1:T(8,128)(2,1)}) %all-gather.5.cloned.1.call-update) | async-done | bytes 1572880 | tf_op jit(solution)/shard_map/all_gather | solution.py:33
  198.5 5.0 %copy.20 = bf16[16,768,64]{1,2,0:T(8,128)(2,1)} copy(bf16[16,768,64]{2,0,1:T(8,128)(2,1)} %all-gather.5.cloned.1.call-done) | data formatting | bytes 3145728 | tf_op jit(solution)/shard_map/all_gather | solution.py:33
  203.5 12.8 %convert_bitcast_fusion = bf16[4,16,16,1024]{3,2,0,1:T(8,128)(2,1)S(1)} fusion(bf16[16,768,4,16]{1,3,2,0:T(8,128)(2,1)} %bitcast.73, bf16[16,1024,768]{2,1,0:T(8,128)(2,1)} %param.13), kind=kOutput, calls=%fused_computation.9 | convolution fusion | flops 1611661312 | bytes 28835840 | tf_op jit(solution)/shard_map/lfsc,ldf->slcd/dot_general | solution.py:35
  216.4 1.5 copy.21
  217.9 4.6 %all-to-all-start.1 = ((bf16[4,16,16,1024]{3,2,1,0:T(8,128)(2,1)}), bf16[4,16,16,1024]{3,2,1,0:T(8,128)(2,1)S(1)}, u32[]{:S(2)}, u32[]{:S(2)}) async-start(bf16[4,16,16,1024]{3,2,1,0:T(8,128)(2,1)} %copy.21), calls=%async_computation.1 | async-start | bytes 4194304 | tf_op jit(solution)/shard_map/all_to_all | solution.py:38
  222.5 0.1 copy.25
  222.6 48.5 %all-to-all-done.1 = bf16[4,16,16,1024]{3,2,1,0:T(8,128)(2,1)S(1)} async-done(((bf16[4,16,16,1024]{3,2,1,0:T(8,128)(2,1)}), bf16[4,16,16,1024]{3,2,1,0:T(8,128)(2,1)S(1)}, u32[]{:S(2)}, u32[]{:S(2)}) %all-to-all-start.1) | async-done | bytes 2097184 | tf_op jit(solution)/shard_map/all_to_all | solution.py:38
  271.1 2.0 gather_fusion.1
  273.2 0.4 fusion.20
  273.6 0.7 copy.30
  (14 shorter events, 0.1 us)
Async XLA Ops:
  6.5 132.0 %all-gather.3.cloned.1.call-start = ((), (), s32[]{:S(2)}) async-start(), calls=%async_computation.2 | async-start | bytes 10485760 | tf_op jit(solution)/shard_map/all_gather | solution.py:61
  80.9 117.6 %all-gather.5.cloned.1.call-start = ((), (), s32[]{:S(2)}) async-start(), calls=%async_computation.3 | async-start | bytes 3932160 | tf_op jit(solution)/shard_map/all_gather | solution.py:33
  216.3 6.2 %copy-start = (f32[64,8]{0,1:T(8,128)S(1)}, f32[64,8]{0,1:T(8,128)}, u32[]{:S(2)}) copy-start(f32[64,8]{0,1:T(8,128)} %param.10) | copy-start | bytes 6148
  217.9 53.2 %all-to-all-start.1 = ((bf16[4,16,16,1024]{3,2,1,0:T(8,128)(2,1)}), bf16[4,16,16,1024]{3,2,1,0:T(8,128)(2,1)S(1)}, u32[]{:S(2)}, u32[]{:S(2)}) async-start(bf16[4,16,16,1024]{3,2,1,0:T(8,128)(2,1)} %copy.21), calls=%async_computation.1 | async-start | bytes 4194304 | tf_op jit(solution)/shard_map/all_to_all | solution.py:38
Sparse Core Ops, SparseCore 0:
  81.0 57.4 all-gather.2
  169.9 28.5 all-gather.4
where the time goes:
time: 282 us; the launch traced here: 281 us
  waiting for transfers between devices  135 us (48%)
  blocking collectives  60 us (21%)
  matrix products  43.1 us (15%)
  local copies, waits for them, and re-layouts  21 us (7%)
  between operations  13.5 us (5%)
  starting transfers between devices  4.82 us (2%)
  other arithmetic  4.13 us (1%)
    all_gather x1, waiting for transfers between devices, body(): lax.all_gather(lax.all_to_all(dispatched, 'expert', split_axis=0, concat_...  57.4 us
    all_to_all x1, blocking collectives, body(): lax.all_to_all(dispatched, 'expert', split_axis=0, concat_axis=0, tiled=T...  51.7 us
    all_to_all x1, waiting for transfers between devices, expert_block(): lax.all_to_all(result, 'expert', split_axis=0, concat_axis=0, tiled=True)  48.5 us
    all_gather x1, waiting for transfers between devices, expert_block(): hidden_all = lax.all_gather(hidden, 'tensor', axis=1, tiled=True)  28.7 us
    dot_general x1, matrix products, expert_block(): jnp.einsum('slcd,lfd->lfsc', slot_rows, up_proj, preferred_element_type=j...  15 us
    dot_general x1, matrix products, expert_block(): jnp.einsum('slcd,lfd->lfsc', slot_rows, gate_proj, preferred_element_type...  14.8 us
    dot_general x1, matrix products, expert_block(): jnp.einsum('lfsc,ldf->slcd', hidden_all, down_proj, preferred_element_typ...  12.8 us
    psum x1, blocking collectives, body(): squares = lax.psum(jnp.sum(values * values, axis=1), 'tensor')  8.34 us
  transfers between devices with their start and end apart: 3, of which 3 were waited for; matrix products, arithmetic and copies ran while one was open for 0% of the time, Pallas kernels for 0%

commit v1 on v0

v1 whole, which is shorter than its diff:
```python
import jax
import jax.numpy as jnp
from jax import lax
from jax.sharding import PartitionSpec as P

D = 4096
EXPERTS = 64
TOP = 8
CAP = 16


epsilon = 1e-06


def earlier_namings(member):
    count = member.shape[-2]
    earlier = jnp.arange(count)[:, None] > jnp.arange(count)[None, :]
    return jnp.einsum(
        "ts,...se->...te",
        earlier.astype(jnp.bfloat16),
        member.astype(jnp.bfloat16),
        preferred_element_type=jnp.float32,
    ).astype(jnp.int32)


def slot_places(expert_ids):
    hit = expert_ids[:, :, None] == jnp.arange(EXPERTS, dtype=jnp.int32)
    before = earlier_namings(jnp.any(hit, axis=1))
    inside = jnp.sum(jnp.where(hit, before[:, None, :], 0), axis=2)
    return (expert_ids * CAP + inside).reshape(-1)


def norm_rows(tokens, norm_gain):
    values = tokens.astype(jnp.float32)
    squares = lax.psum(jnp.sum(values * values, axis=1), "tensor")
    inv_scale = lax.rsqrt(squares / D + epsilon)[:, None]
    width = tokens.shape[1]
    gain_part = lax.dynamic_slice_in_dim(norm_gain, lax.axis_index("tensor") * width, width)
    return (values * inv_scale * gain_part).astype(jnp.bfloat16)


def dispatch_form(tokens, norm_gain, expert_ids, gate_weights, gate_proj, up_proj, down_proj):
    local_experts = gate_proj.shape[0]
    groups = lax.axis_size("expert")
    tok_rows, width = tokens.shape
    places = slot_places(expert_ids)
    owners = (
        jnp.full((EXPERTS * CAP,), tok_rows, jnp.int32)
        .at[places]
        .set(jnp.arange(places.shape[0], dtype=jnp.int32) // TOP)
    )
    normed = norm_rows(tokens, norm_gain)
    padded = jnp.concatenate([normed, jnp.zeros((1, width), jnp.bfloat16)], axis=0)
    dispatched = padded[owners].reshape(groups, local_experts, CAP, width)
    slot_rows = lax.all_gather(
        lax.all_to_all(dispatched, "expert", split_axis=0, concat_axis=0, tiled=True),
        "tensor",
        axis=3,
        tiled=True,
    )
    gate_act = jnp.einsum(
        "slcd,lfd->lfsc", slot_rows, gate_proj, preferred_element_type=jnp.float32
    )
    up_act = jnp.einsum("slcd,lfd->lfsc", slot_rows, up_proj, preferred_element_type=jnp.float32)
    hidden = (jax.nn.silu(gate_act) * up_act).astype(jnp.bfloat16)
    hidden = hidden.reshape(local_experts, hidden.shape[1], groups * CAP)
    hidden_all = lax.all_gather(hidden, "tensor", axis=1, tiled=True)
    hidden_all = hidden_all.reshape(local_experts, hidden_all.shape[1], groups, CAP)
    result = jnp.einsum(
        "lfsc,ldf->slcd", hidden_all, down_proj, preferred_element_type=jnp.float32
    ).astype(jnp.bfloat16)
    returned = lax.all_to_all(result, "expert", split_axis=0, concat_axis=0, tiled=True)
    flat_back = returned.reshape(EXPERTS * CAP, returned.shape[-1])
    picked = flat_back[places].reshape(tok_rows, TOP, -1).astype(jnp.float32)
    return jnp.einsum("tkd,tk->td", picked, gate_weights).astype(jnp.bfloat16)


def gather_form(tokens, norm_gain, expert_ids, gate_weights, gate_proj, up_proj, down_proj):
    local_experts = gate_proj.shape[0]
    groups = lax.axis_size("expert")
    tok_rows = tokens.shape[0]
    ids = lax.all_gather(expert_ids, "expert", axis=0)
    weights = lax.all_gather(gate_weights, "expert", axis=0)
    mine = lax.axis_index("expert") * local_experts + jnp.arange(local_experts, dtype=jnp.int32)
    hit = ids[..., None] == mine
    member = jnp.any(hit, axis=2)
    weight = jnp.sum(jnp.where(hit, weights[..., None], 0.0), axis=2)
    slot = earlier_namings(member) + CAP * jnp.arange(groups)[:, None, None]
    slot = jnp.where(member, slot, -1).reshape(groups * tok_rows, local_experts)
    weight = weight.reshape(groups * tok_rows, local_experts)
    place = slot.T[:, None, :] == jnp.arange(groups * CAP, dtype=jnp.int32)[None, :, None]
    slot_weight = jnp.sum(jnp.where(place, weight.T[:, None, :], 0.0), axis=2)
    place = place.astype(jnp.bfloat16)
    normed = norm_rows(tokens, norm_gain)
    rows = lax.all_gather(lax.all_gather(normed, "expert", axis=0, tiled=True), "tensor", axis=1, tiled=True)
    slot_rows = jnp.einsum("lst,td->lsd", place, rows, preferred_element_type=jnp.float32).astype(jnp.bfloat16)
    gate_act = jnp.einsum("lsd,lfd->lsf", slot_rows, gate_proj, preferred_element_type=jnp.float32)
    up_act = jnp.einsum("lsd,lfd->lsf", slot_rows, up_proj, preferred_element_type=jnp.float32)
    hidden = (jax.nn.silu(gate_act) * up_act).astype(jnp.bfloat16)
    hidden_all = lax.all_gather(hidden, "tensor", axis=2, tiled=True)
    result = jnp.einsum("lsf,ldf->lsd", hidden_all, down_proj, preferred_element_type=jnp.float32)
    result = (result * slot_weight[:, :, None]).astype(jnp.bfloat16)
    partial = jnp.einsum("lst,lsd->td", place, result, preferred_element_type=jnp.float32)
    partial = partial.astype(jnp.bfloat16).reshape(groups, tok_rows, -1)
    parts = lax.all_to_all(partial, "expert", split_axis=0, concat_axis=0, tiled=True)
    return jnp.sum(parts.astype(jnp.float32), axis=0).astype(jnp.bfloat16)


def body(tokens, norm_gain, expert_ids, gate_weights, gate_proj, up_proj, down_proj):
    form = gather_form if tokens.shape[0] < gate_proj.shape[0] * CAP else dispatch_form
    return form(tokens, norm_gain, expert_ids, gate_weights, gate_proj, up_proj, down_proj)


def solution(mesh):
    return jax.shard_map(
        body,
        mesh=mesh,
        in_specs=(
            P(("group", "expert"), "tensor"),
            P(),
            P(("group", "expert"), None),
            P(("group", "expert"), None),
            P("expert", "tensor", None),
            P("expert", "tensor", None),
            P("expert", "tensor", None),
        ),
        out_specs=P(("group", "expert"), "tensor"),
        check_vma=False,
    )
```

time: 282 us -> 166 us (0.59)
  waiting for transfers between devices: 135 us -> 25.1 us
  local copies, waits for them, and re-layouts: 21 us -> 2.43 us
  blocking collectives: 60 us -> 70.4 us
  matrix products: 43.1 us -> 50.7 us
  starting transfers between devices: 4.82 us -> 0.04 us
    all_gather x2, waiting for transfers between devices: 86 us -> 25.1 us  [the longest x1 14.9 us: gather_form(): hidden_all = lax.all_gather(hidden, 'tensor', axis=2, tiled=True)]
    all_to_all x1 -> x0, waiting for transfers between devices: 48.5 us -> none  [expert_block(): lax.all_to_all(result, 'expert', split_axis=0, concat_axis=0, tiled=True)]
    all_gather x0 -> x3, blocking collectives: none -> 42.8 us  [the longest x1 15.8 us: gather_form(): lax.all_gather(normed, 'expert', axis=0, tiled=True)]
    all_to_all x1, blocking collectives: 51.7 us -> 19.3 us  [gather_form(): lax.all_to_all(partial, 'expert', split_axis=0, concat_axis=0, tiled=True)]
    dot_general x4 -> x5, matrix products: 43.1 us -> 50.7 us  [the longest x1 15 us: gather_form(): jnp.einsum('lsd,lfd->lsf', slot_rows, up_proj, preferred_element_type=jnp...]
    gather x2 -> x0, local copies, waits for them, and re-layouts: 6.12 us -> none  [the longest x1 4.07 us: body(): padded[owners].reshape(groups, local_experts, CAP, quarter_width)]
    all_gather x1 -> x0, local copies, waits for them, and re-layouts: 4.99 us -> none  [expert_block(): hidden_all = lax.all_gather(hidden, 'tensor', axis=1, tiled=True)]
    all_to_all x1 -> x0, starting transfers between devices: 4.6 us -> none  [expert_block(): lax.all_to_all(result, 'expert', split_axis=0, concat_axis=0, tiled=True)]
  transfers between devices with their start and end apart: 3 -> 2, of which waited for: 3 -> 2; matrix products, arithmetic and copies ran while one was open for 0% -> 0% of each run, Pallas kernels for 0% -> 0%
where the time goes in v1:
time: 166 us; the launch traced here: 165 us
  blocking collectives  70.4 us (42%)
  matrix products  50.7 us (31%)
  waiting for transfers between devices  25.1 us (15%)
  between operations  13.5 us (8%)
  other arithmetic  3.23 us (2%)
  local copies, waits for them, and re-layouts  2.43 us (1%)
    all_to_all x1, blocking collectives, gather_form(): lax.all_to_all(partial, 'expert', split_axis=0, concat_axis=0, tiled=True)  19.3 us
    all_gather x1, blocking collectives, gather_form(): lax.all_gather(normed, 'expert', axis=0, tiled=True)  15.8 us
    dot_general x1, matrix products, gather_form(): jnp.einsum('lsd,lfd->lsf', slot_rows, up_proj, preferred_element_type=jnp...  15 us
    all_gather x1, waiting for transfers between devices, gather_form(): hidden_all = lax.all_gather(hidden, 'tensor', axis=2, tiled=True)  14.9 us
    dot_general x1, matrix products, gather_form(): jnp.einsum('lsd,lfd->lsf', slot_rows, gate_proj, preferred_element_type=j...  14.8 us
    dot_general x1, matrix products, gather_form(): jnp.einsum('lst,lsd->td', place, result, preferred_element_type=jnp.float32)  13.6 us
    all_gather x1, blocking collectives, gather_form(): ids = lax.all_gather(expert_ids, 'expert', axis=0)  13.6 us
    all_gather x1, blocking collectives, gather_form(): weights = lax.all_gather(gate_weights, 'expert', axis=0)  13.3 us
  transfers between devices with their start and end apart: 2, of which 2 were waited for; matrix products, arithmetic and copies ran while one was open for 0% of the time, Pallas kernels for 0%

profile of v1, /device:TPU:0, one launch (start us, length us, event | category | flops | bytes accessed | tf_op | source)
XLA Modules:
  0.0 165.4 jit_solution(7242551088797172167)
XLA Ops:
  6.5 0.0 all-gather.7.cloned.1.call-start
  6.5 1.0 fusion.21
  7.6 8.3 %psum.7 = f32[64]{0:T(128)S(1)} all-reduce(f32[64]{0:T(128)S(1)} %fusion.21), channel_id=1, replica_groups=mesh['group'=2,'expert'=4,'tensor'=4] {'tensor'}, use_global_device_ids=true, to_apply=%region_2.3 | all-reduce | flops 64 | bytes 512 | tf_op jit(solution)/shard_map/psum | solution.py:35
  15.9 0.7 dynamic_slice.3
  16.6 1.0 fusion.23
  17.6 15.8 %all_gather.23 = bf16[256,1024]{1,0:T(8,128)(2,1)} all-gather(bf16[64,1024]{1,0:T(8,128)(2,1)S(1)} %fusion.23), channel_id=1, replica_groups=mesh['group'=2,'expert'=4,'tensor'=4] {'expert'}, dimensions={0}, use_global_device_ids=true | all-gather | bytes 655360 | tf_op jit(solution)/shard_map/all_gather | solution.py:95
  33.5 0.0 all-gather.7.cloned.1.call-update
  33.5 0.0 all-gather.9.cloned.1.call-start
  33.5 13.6 %all-gather.2 = s32[4,64,8]{1,2,0:T(8,128)S(1)} all-gather(s32[1,64,8]{1,2,0:T(8,128)} %bitcast.34), channel_id=2, replica_groups=mesh['group'=2,'expert'=4,'tensor'=4] {'expert'}, dimensions={0}, use_global_device_ids=true | all-gather | bytes 10240 | tf_op jit(solution)/shard_map/all_gather | solution.py:82
  47.1 0.1 compare_reduce_fusion
  47.3 0.1 fusion.18
  47.3 0.1 copy.21
  47.4 0.1 reshape.25
  47.5 10.2 %all-gather.7.cloned.1.call-done = bf16[256,4096]{1,0:T(8,128)(2,1)} async-done(((bf16[256,1024]{1,0:T(8,128)(2,1)}), bf16[256,4096]{1,0:T(8,128)(2,1)}) %all-gather.7.cloned.1.call-update) | async-done | bytes 2097168 | tf_op jit(solution)/shard_map/all_gather | solution.py:95
  57.7 7.1 %convolution_convert_fusion = bf16[16,64,4096]{2,1,0:T(8,128)(2,1)} fusion(bf16[256,4096]{1,0:T(8,128)(2,1)} %all-gather.7.cloned.1.call-done, s32[16,256]{1,0:T(8,128)S(1)} %bitcast.30), kind=kOutput, calls=%fused_computation | convolution fusion | flops 2151940096 | bytes 10502144 | tf_op jit(solution)/shard_map/lst,td->lsd/dot_general | solution.py:96
  64.8 14.8 %fusion.27 = f32[16,64,192]{2,1,0:T(8,128)S(1)} fusion(bf16[16,64,4096]{2,1,0:T(8,128)(2,1)} %convolution_convert_fusion, bf16[16,192,4096]{2,1,0:T(8,128)(2,1)} %param.11), kind=kOutput, calls=%fused_computation.32 | convolution fusion | flops 1610612736 | bytes 34340864 | tf_op jit(solution)/shard_map/lsd,lfd->lsf/dot_general | solution.py:97
  79.6 0.0 copy-start
  79.6 15.0 %fusion.15 = bf16[16,64,192]{2,1,0:T(8,128)(2,1)S(1)} fusion(bf16[16,64,4096]{2,1,0:T(8,128)(2,1)} %convolution_convert_fusion, bf16[16,192,4096]{2,1,0:T(8,128)(2,1)} %param.12, f32[16,64,192]{2,1,0:T(8,128)S(1)} %fusion.27), kind=kOutput, calls=%fused_computation.10 | convolution fusion | flops 1611792384 | bytes 34734080 | tf_op jit(solution)/shard_map/lsd,lfd->lsf/dot_general | solution.py:98
  94.7 1.5 copy.22
  96.1 0.0 all-gather.9.cloned.1.call-update
  96.2 0.0 copy-done
  96.2 13.3 %all-gather.3 = f32[4,64,8]{1,2,0:T(8,128)S(1)} all-gather(f32[1,64,8]{1,2,0:T(8,128)S(1)} %bitcast.35), channel_id=3, replica_groups=mesh['group'=2,'expert'=4,'tensor'=4] {'expert'}, dimensions={0}, use_global_device_ids=true | all-gather | bytes 10240 | tf_op jit(solution)/shard_map/all_gather | solution.py:83
  109.5 0.1 fusion.24
  109.7 0.1 reshape.26
  109.7 0.2 select_reduce_fusion
  110.0 14.9 %all-gather.9.cloned.1.call-done = bf16[16,64,768]{1,0,2:T(8,128)(2,1)} async-done(((bf16[16,64,192]{1,0,2:T(8,128)(2,1)}), bf16[16,64,768]{1,0,2:T(8,128)(2,1)}) %all-gather.9.cloned.1.call-update) | async-done | bytes 1572880 | tf_op jit(solution)/shard_map/all_gather | solution.py:100
  124.9 13.6 %fusion.12 = bf16[256,1024]{1,0:T(8,128)(2,1)S(1)} fusion(bf16[16,1024,768]{2,1,0:T(8,128)(2,1)} %param.13, bf16[16,64,768]{1,0,2:T(8,128)(2,1)} %all-gather.9.cloned.1.call-done, f32[16,64]{1,0:T(8,128)S(1)} %select_reduce_fusion, s32[16,256]{1,0:T(8,128)S(1)} %bitcast.32), kind=kOutput, calls=%fused_computation.9 | convolution fusion | flops 2150105088 | bytes 27283456 | tf_op jit(solution)/shard_map/lst,lsd->td/dot_general | solution.py:103
  138.5 19.3 %all_to_all.5 = bf16[4,64,1024]{2,1,0:T(8,128)(2,1)S(1)} all-to-all(bf16[4,64,1024]{2,1,0:T(8,128)(2,1)S(1)} %bitcast.29), channel_id=1, replica_groups=mesh['group'=2,'expert'=4,'tensor'=4] {'expert'}, dimensions={0} | all-to-all | bytes 1048576 | tf_op jit(solution)/shard_map/all_to_all | solution.py:105
  157.8 0.7 reduce_sum.42
  (4 shorter events, 0.0 us)
Async XLA Ops:
  6.5 51.1 %all-gather.7.cloned.1.call-start = ((), (), s32[]{:S(2)}) async-start(), calls=%async_computation.1 | async-start | bytes 2621440 | tf_op jit(solution)/shard_map/all_gather | solution.py:95
  33.5 91.4 %all-gather.9.cloned.1.call-start = ((), (), s32[]{:S(2)}) async-start(), calls=%async_computation.2 | async-start | bytes 3932160 | tf_op jit(solution)/shard_map/all_gather | solution.py:100
  79.6 16.6 %copy-start = (f32[64,8]{0,1:T(8,128)S(1)}, f32[64,8]{0,1:T(8,128)}, u32[]{:S(2)}) copy-start(f32[64,8]{0,1:T(8,128)} %param.10) | copy-start | bytes 6148
Sparse Core Ops, SparseCore 0:
  33.6 24.0 all-gather.6
  96.3 28.5 all-gather.8

commit v2 on v1

--- a/solution.py
+++ b/solution.py
@@ -1,6 +1,8 @@
 import jax
 import jax.numpy as jnp
 from jax import lax
+from jax.experimental import pallas as pl
+from jax.experimental.pallas import tpu as pltpu
 from jax.sharding import PartitionSpec as P
 
 D = 4096
@@ -106,8 +108,247 @@
     return jnp.sum(parts.astype(jnp.float32), axis=0).astype(jnp.bfloat16)
 
 
+NT = (((1,), (1,)), ((), ()))
+MESH = pl.DeviceIdType.MESH
+
+
+def kernel(
+    tok_ref, gain_ref, ids_ref, gw_ref, gate_ref, up_ref, down_ref, out_ref,
+    raw, xn, info, gu, dn, hid, acc, parts, back,
+    gu_sem, dn_sem, tok_send, tok_recv, info_send, info_recv, hid_send, hid_recv, part_send, part_recv,
+):
+    experts, units, _ = gate_ref.shape
+    rows, width = tok_ref.shape
+    groups, shards = info.shape[0], raw.shape[0]
+    total, pairs = groups * rows, experts // 2
+    lanes = info.shape[-1]
+    deep_gu, deep_dn = gu.shape[0], dn.shape[0]
+    half = groups * CAP
+    z, t = lax.axis_index("expert"), lax.axis_index("tensor")
+    mate, across, diagonal = t + 1 - 2 * (t % 2), (t + 2) % 4, 3 - t
+
+    def weights(e, slot):
+        return [
+            pltpu.make_async_copy(gate_ref.at[e], gu.at[slot, 0], gu_sem.at[slot, 0]),
+            pltpu.make_async_copy(up_ref.at[e], gu.at[slot, 1], gu_sem.at[slot, 1]),
+        ]
+
+    def downs(e, slot):
+        return pltpu.make_async_copy(down_ref.at[e], dn.at[slot], dn_sem.at[slot])
+
+    def send(src, dst, ss, rs, **to):
+        return pltpu.make_async_remote_copy(
+            src_ref=src, dst_ref=dst, send_sem=ss, recv_sem=rs, device_id=to, device_id_type=MESH
+        )
+
+    for e in range(deep_gu):
+        for c in weights(e, e):
+            c.start()
+    for e in range(deep_dn):
+        downs(e, e).start()
+
+    barrier = pltpu.get_barrier_semaphore()
+    for d in range(1, groups):
+        pl.semaphore_signal(barrier, inc=1, device_id={"expert": (z + d) % groups}, device_id_type=MESH)
+    for peer in (mate, across, diagonal):
+        pl.semaphore_signal(barrier, inc=1, device_id={"tensor": peer}, device_id_type=MESH)
+    pl.semaphore_wait(barrier, groups + 2)
+
+    def block(shard, d):
+        return raw.at[shard, pl.ds(pl.multiple_of((z + groups - d) % groups * rows, rows), rows)]
+
+    first = [
+        send(tok_ref, block(t, 0), tok_send.at[0, d], tok_recv.at[0, d], expert=(z + d) % groups)
+        for d in range(1, groups)
+    ]
+    for c in first:
+        c.start()
+    raw[t, pl.ds(pl.multiple_of(z * rows, rows), rows), :] = tok_ref[...]
+    over = [send(block(t, d), block(t, d), tok_send.at[1, d], tok_recv.at[1, d], tensor=across) for d in range(groups)]
+    near = [send(block(t, d), block(t, d), tok_send.at[2, d], tok_recv.at[2, d], tensor=mate) for d in range(groups)]
+    on = [
+        send(block(across, d), block(across, d), tok_send.at[3, d], tok_recv.at[3, d], tensor=mate)
+        for d in range(groups)
+    ]
+    over[0].start()
+    near[0].start()
+
+    lane = lax.broadcasted_iota(jnp.int32, (rows, lanes), 1)
+    member = jnp.zeros((rows, lanes), jnp.float32)
+    weight = jnp.zeros((rows, lanes), jnp.float32)
+    for k in range(ids_ref.shape[1]):
+        hit = ids_ref[:, k : k + 1] == lane
+        member = jnp.where(hit, 1.0, member)
+        weight = jnp.where(hit, gw_ref[:, k : k + 1], weight)
+    earlier = lax.broadcasted_iota(jnp.int32, (rows, rows), 0) > lax.broadcasted_iota(jnp.int32, (rows, rows), 1)
+    before = jnp.dot(
+        jnp.where(earlier, 1.0, 0.0).astype(jnp.bfloat16),
+        member.astype(jnp.bfloat16),
+        preferred_element_type=jnp.float32,
+    )
+    info[z, 0] = jnp.where(member > 0, before + (z * CAP).astype(jnp.float32), -1000.0)
+    info[z, 1] = weight
+    told = [
+        send(info.at[z], info.at[z], info_send.at[d], info_recv.at[d], expert=(z + d) % groups)
+        for d in range(1, groups)
+    ]
+    for c in told:
+        c.start()
+
+    for d in range(1, groups):
+        first[d - 1].wait_recv()
+        over[d].start()
+        near[d].start()
+    for d in range(groups):
+        over[d].wait_recv()
+        on[d].start()
+    for c in told:
+        c.wait_recv()
+    for d in range(groups):
+        near[d].wait_recv()
+        on[d].wait_recv()
+
+    step = 32
+
+    @pl.loop(0, total // step)
+    def _(r):
+        at = pl.ds(pl.multiple_of(r * step, step), step)
+        values = [raw[s, at, :].astype(jnp.float32) for s in range(shards)]
+        squares = sum(jnp.sum(v * v, axis=1, keepdims=True) for v in values)
+        inv_scale = lax.rsqrt(squares / (shards * width) + epsilon)
+        for s in range(shards):
+            xn[s, at, :] = (values[s] * inv_scale * gain_ref[s : s + 1, :]).astype(jnp.bfloat16)
+
+    def column(which, e):
+        table = info[:, which].reshape(total, lanes)
+        here = lax.broadcasted_iota(jnp.int32, (total, lanes), 1) == z * experts + e
+        return jnp.sum(jnp.where(here, table, 0.0), axis=1, keepdims=True)
+
+    def place(e, side):
+        at = lax.broadcasted_iota(jnp.int32, (total, 2 * half), 1).astype(jnp.float32)
+        return jnp.where(column(0, e) + float(side * half) == at, 1.0, 0.0).astype(jnp.bfloat16)
+
+    def part_of_hidden(p):
+        return hid.at[p, pl.ds(pl.multiple_of(t * units, units), units)]
+
+    def tell(p):
+        return [
+            send(part_of_hidden(p), part_of_hidden(p), hid_send.at[p, i], hid_recv.at[p, i], tensor=peer)
+            for i, peer in enumerate((mate, across, diagonal))
+        ]
+
+    @pl.loop(0, pairs)
+    def _(p):
+        both = jnp.zeros((units, 2 * half), jnp.float32)
+        for side in range(2):
+            e = 2 * p + side
+            slot = e % deep_gu
+            for c in weights(e, slot):
+                c.wait()
+            acts = []
+            for m in range(2):
+                act = jnp.zeros((units, total), jnp.float32)
+                for s in range(shards):
+                    act += lax.dot_general(
+                        gu[slot, m, :, s * width : (s + 1) * width], xn[s], NT, preferred_element_type=jnp.float32
+                    )
+                acts.append(act)
+
+            @pl.when(e + deep_gu < experts)
+            def _():
+                for c in weights(e + deep_gu, slot):
+                    c.start()
+
+            hidden = (acts[0] / (1.0 + jnp.exp(-acts[0])) * acts[1]).astype(jnp.bfloat16)
+            both += jnp.dot(hidden, place(e, side), preferred_element_type=jnp.float32)
+        hid[p, pl.ds(pl.multiple_of(t * units, units), units), :] = both.astype(jnp.bfloat16)
+        for c in tell(p):
+            c.start()
+
+    acc[...] = jnp.zeros_like(acc)
+
+    @pl.loop(0, pairs)
+    def _(p):
+        for c in tell(p):
+            c.wait()
+        for side in range(2):
+            e = 2 * p + side
+            slot = e % deep_dn
+            downs(e, slot).wait()
+            spread = lax.dot_general(place(e, side), hid[p], NT, preferred_element_type=jnp.float32)
+            spread = (spread * column(1, e)).astype(jnp.bfloat16)
+            acc[...] += lax.dot_general(spread, dn[slot], NT, preferred_element_type=jnp.float32)
+
+            @pl.when(e + deep_dn < experts)
+            def _():
+                downs(e + deep_dn, slot).start()
+
+    for b in range(groups):
+        parts[b] = acc[b * rows : (b + 1) * rows, :].astype(jnp.bfloat16)
+    shares = [
+        send(parts.at[(z + d) % groups], back.at[d], part_send.at[d], part_recv.at[d], expert=(z + d) % groups)
+        for d in range(1, groups)
+    ]
+    for c in shares:
+        c.start()
+    result = acc[pl.ds(pl.multiple_of(z * rows, rows), rows), :]
+    for d, c in enumerate(shares, 1):
+        c.wait_recv()
+        result += back[d].astype(jnp.float32)
+    out_ref[...] = result.astype(jnp.bfloat16)
+    for c in first + over + near + on + told + shares:
+        c.wait_send()
+
+
+def kernel_form(tokens, norm_gain, expert_ids, gate_weights, gate_proj, up_proj, down_proj):
+    groups, shards = lax.axis_size("expert"), lax.axis_size("tensor")
+    rows, width = tokens.shape
+    experts, units, features = gate_proj.shape
+    out_width = down_proj.shape[1]
+    total, pairs, lanes = groups * rows, experts // 2, -(-EXPERTS // 128) * 128
+    deep_gu, deep_dn = min(experts, 8), min(experts, 10)
+    vmem, hbm = pl.BlockSpec(memory_space=pltpu.VMEM), pl.BlockSpec(memory_space=pl.ANY)
+    dma = pltpu.SemaphoreType.DMA
+    flops = 2 * total * experts * (2 * units * features + out_width * down_proj.shape[2])
+    return pl.pallas_call(
+        kernel,
+        out_shape=jax.ShapeDtypeStruct((rows, out_width), jnp.bfloat16),
+        in_specs=[vmem] * 4 + [hbm] * 3,
+        out_specs=vmem,
+        scratch_shapes=[
+            pltpu.VMEM((shards, total, width), jnp.bfloat16),
+            pltpu.VMEM((shards, total, width), jnp.bfloat16),
+            pltpu.VMEM((groups, 2, rows, lanes), jnp.float32),
+            pltpu.VMEM((deep_gu, 2, units, features), jnp.bfloat16),
+            pltpu.VMEM((deep_dn,) + down_proj.shape[1:], jnp.bfloat16),
+            pltpu.VMEM((pairs, shards * units, 2 * groups * CAP), jnp.bfloat16),
+            pltpu.VMEM((total, out_width), jnp.float32),
+            pltpu.VMEM((groups, rows, out_width), jnp.bfloat16),
+            pltpu.VMEM((groups, rows, out_width), jnp.bfloat16),
+            dma((deep_gu, 2)),
+            dma((deep_dn,)),
+            dma((4, groups)),
+            dma((4, groups)),
+            dma((groups,)),
+            dma((groups,)),
+            dma((pairs, 3)),
+            dma((pairs, 3)),
+            dma((groups,)),
+            dma((groups,)),
+        ],
+        compiler_params=pltpu.CompilerParams(
+            collective_id=0, has_side_effects=True, vmem_limit_bytes=58 * 2**20
+        ),
+        cost_estimate=pl.CostEstimate(flops=flops, bytes_accessed=3 * 2 * gate_proj.size, transcendentals=0),
+    )(tokens, norm_gain.reshape(shards, width), expert_ids, gate_weights, gate_proj, up_proj, down_proj)
+
+
 def body(tokens, norm_gain, expert_ids, gate_weights, gate_proj, up_proj, down_proj):
-    form = gather_form if tokens.shape[0] < gate_proj.shape[0] * CAP else dispatch_form
+    form = dispatch_form
+    if tokens.shape[0] < gate_proj.shape[0] * CAP:
+        form = gather_form
+        if lax.axis_size("tensor") == 4 and gate_proj.shape[0] % 2 == 0:
+            form = kernel_form
     return form(tokens, norm_gain, expert_ids, gate_weights, gate_proj, up_proj, down_proj)
 
 

time: 166 us -> 83.2 us (0.50)
  the two profiles are of different devices: /device:TPU:0 before, /device:TPU:25 now
where the time goes in v2:
time: 83.2 us; the launch traced here: 82.9 us
  Pallas kernels  77.3 us (93%)
  local copies, waits for them, and re-layouts  5.64 us (7%)
    pallas_call x1, Pallas kernels, kernel_form(): pl.pallas_call(kernel, out_shape=jax.ShapeDtypeStruct((rows, out_width),...  77.3 us
    unnamed x3, local copies, waits for them, and re-layouts  4.32 us

profile of v2, /device:TPU:25, one launch (start us, length us, event | category | flops | bytes accessed | tf_op | source)
XLA Modules:
  0.0 82.9 jit_solution(7747627516732391804)
XLA Ops:
  0.0 1.3 %reshape.3.gain_ref = f32[4,1024]{1,0:T(4,128)} reshape(f32[4096]{0:T(1024)} %param.8) | data formatting | bytes 32768 | tf_op jit(solution)/shard_map/reshape | solution.py:343
  1.3 1.4 %copy.8.ids_ref = s32[64,8]{1,0:T(8,128)} copy(s32[64,8]{0,1:T(8,128)} %param.9) | data formatting | bytes 4096 | tf_op args[2]
  2.7 1.4 %copy.9.gw_ref = f32[64,8]{1,0:T(8,128)} copy(f32[64,8]{0,1:T(8,128)} %param.10) | data formatting | bytes 4096 | tf_op args[3]
  4.1 77.3 %shard_map.73 = bf16[64,1024]{1,0:T(8,128)(2,1)} custom-call(bf16[64,1024]{1,0:T(8,128)(2,1)} %tok_ref.1, f32[4,1024]{1,0:T(4,128)} %reshape.3.gain_ref, s32[64,8]{1,0:T(8,128)} %copy.8.ids_ref, f32[64,8]{1,0:T(8,128)} %copy.9.gw_ref, bf16[16,192,4096]{2,1,0:T(8,128)(2,1)} %gate_ref.1, bf16[16,192,4096]{2,1,0:T(8,128)(2,1)} %up_ref.1, ...), custom_call_target="tpu_custom_call" | custom-call | flops 19327352832 | bytes 75497472 | tf_op jit(solution)/shard_map/pallas_call | solution.py:313
  81.4 1.6 %copy.11 = bf16[64,1024]{1,0:T(8,128)(2,1)} copy(bf16[64,1024]{1,0:T(8,128)(2,1)} %shard_map.73) | data formatting | bytes 262144

commit v3 on v2

--- a/solution.py
+++ b/solution.py
@@ -114,7 +114,7 @@
 
 def kernel(
     tok_ref, gain_ref, ids_ref, gw_ref, gate_ref, up_ref, down_ref, out_ref,
-    raw, xn, info, gu, dn, hid, acc, parts, back,
+    raw, xn, info, gu, dn, hid, spread, acc, parts, back,
     gu_sem, dn_sem, tok_send, tok_recv, info_send, info_recv, hid_send, hid_recv, part_send, part_recv,
 ):
     experts, units, _ = gate_ref.shape
@@ -127,14 +127,26 @@
     z, t = lax.axis_index("expert"), lax.axis_index("tensor")
     mate, across, diagonal = t + 1 - 2 * (t % 2), (t + 2) % 4, 3 - t
 
-    def weights(e, slot):
+    depth, part = down_ref.shape[2], acc.shape[2]
+
+    def weights(p, slot):
         return [
-            pltpu.make_async_copy(gate_ref.at[e], gu.at[slot, 0], gu_sem.at[slot, 0]),
-            pltpu.make_async_copy(up_ref.at[e], gu.at[slot, 1], gu_sem.at[slot, 1]),
+            pltpu.make_async_copy(ref.at[2 * p + side], gu.at[slot, side, m], gu_sem.at[slot, side, m])
+            for side in range(2)
+            for m, ref in enumerate((gate_ref, up_ref))
         ]
 
-    def downs(e, slot):
-        return pltpu.make_async_copy(down_ref.at[e], dn.at[slot], dn_sem.at[slot])
+    def downs(unit, slot):
+        h, p = unit // pairs, unit % pairs
+        features = pl.ds(pl.multiple_of(h * part, part), part)
+        return [
+            pltpu.make_async_copy(
+                down_ref.at[2 * p + side, features],
+                dn.at[slot, :, pl.ds(side * depth, depth)],
+                dn_sem.at[slot, side],
+            )
+            for side in range(2)
+        ]
 
     def send(src, dst, ss, rs, **to):
         return pltpu.make_async_remote_copy(
@@ -145,7 +157,8 @@
         for c in weights(e, e):
             c.start()
     for e in range(deep_dn):
-        downs(e, e).start()
+        for c in downs(e, e):
+            c.start()
 
     barrier = pltpu.get_barrier_semaphore()
     for d in range(1, groups):
@@ -217,7 +230,7 @@
         squares = sum(jnp.sum(v * v, axis=1, keepdims=True) for v in values)
         inv_scale = lax.rsqrt(squares / (shards * width) + epsilon)
         for s in range(shards):
-            xn[s, at, :] = (values[s] * inv_scale * gain_ref[s : s + 1, :]).astype(jnp.bfloat16)
+            xn[at, s * width : (s + 1) * width] = (values[s] * inv_scale * gain_ref[s : s + 1, :]).astype(jnp.bfloat16)
 
     def column(which, e):
         table = info[:, which].reshape(total, lanes)
@@ -239,64 +252,72 @@
 
     @pl.loop(0, pairs)
     def _(p):
+        slot = p % deep_gu
+        for c in weights(p, slot):
+            c.wait()
+        acts = lax.dot_general(
+            gu[slot].reshape(4 * units, shards * width), xn[...], NT, preferred_element_type=jnp.float32
+        )
+
+        @pl.when(p + deep_gu < pairs)
+        def _():
+            for c in weights(p + deep_gu, slot):
+                c.start()
+
         both = jnp.zeros((units, 2 * half), jnp.float32)
         for side in range(2):
-            e = 2 * p + side
-            slot = e % deep_gu
-            for c in weights(e, slot):
-                c.wait()
-            acts = []
-            for m in range(2):
-                act = jnp.zeros((units, total), jnp.float32)
-                for s in range(shards):
-                    act += lax.dot_general(
-                        gu[slot, m, :, s * width : (s + 1) * width], xn[s], NT, preferred_element_type=jnp.float32
-                    )
-                acts.append(act)
-
-            @pl.when(e + deep_gu < experts)
-            def _():
-                for c in weights(e + deep_gu, slot):
-                    c.start()
-
-            hidden = (acts[0] / (1.0 + jnp.exp(-acts[0])) * acts[1]).astype(jnp.bfloat16)
-            both += jnp.dot(hidden, place(e, side), preferred_element_type=jnp.float32)
+            gate = acts[2 * side * units : (2 * side + 1) * units]
+            up = acts[(2 * side + 1) * units : (2 * side + 2) * units]
+            hidden = (gate / (1.0 + jnp.exp(-gate)) * up).astype(jnp.bfloat16)
+            both += jnp.dot(hidden, place(2 * p + side, side), preferred_element_type=jnp.float32)
         hid[p, pl.ds(pl.multiple_of(t * units, units), units), :] = both.astype(jnp.bfloat16)
         for c in tell(p):
             c.start()
 
-    acc[...] = jnp.zeros_like(acc)
-
-    @pl.loop(0, pairs)
-    def _(p):
-        for c in tell(p):
-            c.wait()
-        for side in range(2):
-            e = 2 * p + side
-            slot = e % deep_dn
-            downs(e, slot).wait()
-            spread = lax.dot_general(place(e, side), hid[p], NT, preferred_element_type=jnp.float32)
-            spread = (spread * column(1, e)).astype(jnp.bfloat16)
-            acc[...] += lax.dot_general(spread, dn[slot], NT, preferred_element_type=jnp.float32)
-
-            @pl.when(e + deep_dn < experts)
+    def shares(h):
+        return [
+            send(
+                parts.at[h, (z + d) % groups], back.at[h, d], part_send.at[h, d], part_recv.at[h, d],
+                expert=(z + d) % groups,
+            )
+            for d in range(1, groups)
+        ]
+
+    for h in range(2):
+        acc[h] = jnp.zeros_like(acc[h])
+
+        @pl.loop(0, pairs)
+        def _(p):
+            if h == 0:
+                for c in tell(p):
+                    c.wait()
+                for side in range(2):
+                    e = 2 * p + side
+                    rows_of = lax.dot_general(place(e, side), hid[p], NT, preferred_element_type=jnp.float32)
+                    spread[p, :, side * depth : (side + 1) * depth] = (rows_of * column(1, e)).astype(jnp.bfloat16)
+            unit = h * pairs + p
+            slot = unit % deep_dn
+            for c in downs(unit, slot):
+                c.wait()
+            acc[h] += lax.dot_general(spread[p], dn[slot], NT, preferred_element_type=jnp.float32)
+
+            @pl.when(unit + deep_dn < 2 * pairs)
             def _():
-                downs(e + deep_dn, slot).start()
-
-    for b in range(groups):
-        parts[b] = acc[b * rows : (b + 1) * rows, :].astype(jnp.bfloat16)
-    shares = [
-        send(parts.at[(z + d) % groups], back.at[d], part_send.at[d], part_recv.at[d], expert=(z + d) % groups)
-        for d in range(1, groups)
-    ]
-    for c in shares:
-        c.start()
-    result = acc[pl.ds(pl.multiple_of(z * rows, rows), rows), :]
-    for d, c in enumerate(shares, 1):
-        c.wait_recv()
-        result += back[d].astype(jnp.float32)
-    out_ref[...] = result.astype(jnp.bfloat16)
-    for c in first + over + near + on + told + shares:
+                for c in downs(unit + deep_dn, slot):
+                    c.start()
+
+        for b in range(groups):
+            parts[h, b] = acc[h, b * rows : (b + 1) * rows, :].astype(jnp.bfloat16)
+        for c in shares(h):
+            c.start()
+
+    for h in range(2):
+        result = acc[h, pl.ds(pl.multiple_of(z * rows, rows), rows), :]
+        for d, c in enumerate(shares(h), 1):
+            c.wait_recv()
+            result += back[h, d].astype(jnp.float32)
+        out_ref[:, h * part : (h + 1) * part] = result.astype(jnp.bfloat16)
+    for c in first + over + near + on + told + shares(0) + shares(1):
         c.wait_send()
 
 
@@ -306,7 +327,7 @@
     experts, units, features = gate_proj.shape
     out_width = down_proj.shape[1]
     total, pairs, lanes = groups * rows, experts // 2, -(-EXPERTS // 128) * 128
-    deep_gu, deep_dn = min(experts, 8), min(experts, 10)
+    deep_gu, deep_dn, part = min(pairs, 4), min(2 * pairs, 8), out_width // 2
     vmem, hbm = pl.BlockSpec(memory_space=pltpu.VMEM), pl.BlockSpec(memory_space=pl.ANY)
     dma = pltpu.SemaphoreType.DMA
     flops = 2 * total * experts * (2 * units * features + out_width * down_proj.shape[2])
@@ -317,24 +338,25 @@
         out_specs=vmem,
         scratch_shapes=[
             pltpu.VMEM((shards, total, width), jnp.bfloat16),
-            pltpu.VMEM((shards, total, width), jnp.bfloat16),
+            pltpu.VMEM((total, shards * width), jnp.bfloat16),
             pltpu.VMEM((groups, 2, rows, lanes), jnp.float32),
-            pltpu.VMEM((deep_gu, 2, units, features), jnp.bfloat16),
-            pltpu.VMEM((deep_dn,) + down_proj.shape[1:], jnp.bfloat16),
+            pltpu.VMEM((deep_gu, 2, 2, units, features), jnp.bfloat16),
+            pltpu.VMEM((deep_dn, part, 2 * down_proj.shape[2]), jnp.bfloat16),
             pltpu.VMEM((pairs, shards * units, 2 * groups * CAP), jnp.bfloat16),
-            pltpu.VMEM((total, out_width), jnp.float32),
-            pltpu.VMEM((groups, rows, out_width), jnp.bfloat16),
-            pltpu.VMEM((groups, rows, out_width), jnp.bfloat16),
-            dma((deep_gu, 2)),
-            dma((deep_dn,)),
+            pltpu.VMEM((pairs, total, 2 * down_proj.shape[2]), jnp.bfloat16),
+            pltpu.VMEM((2, total, part), jnp.float32),
+            pltpu.VMEM((2, groups, rows, part), jnp.bfloat16),
+            pltpu.VMEM((2, groups, rows, part), jnp.bfloat16),
+            dma((deep_gu, 2, 2)),
+            dma((deep_dn, 2)),
             dma((4, groups)),
             dma((4, groups)),
             dma((groups,)),
             dma((groups,)),
             dma((pairs, 3)),
             dma((pairs, 3)),
-            dma((groups,)),
-            dma((groups,)),
+            dma((2, groups)),
+            dma((2, groups)),
         ],
         compiler_params=pltpu.CompilerParams(
             collective_id=0, has_side_effects=True, vmem_limit_bytes=58 * 2**20

time: 83.2 us -> 72.2 us (0.87)
  the two profiles are of different devices: /device:TPU:25 before, /device:TPU:0 now
where the time goes in v3:
time: 72.2 us; the launch traced here: 71.4 us
  Pallas kernels  65.7 us (91%)
  local copies, waits for them, and re-layouts  5.64 us (8%)
    pallas_call x1, Pallas kernels, kernel_form(): pl.pallas_call(kernel, out_shape=jax.ShapeDtypeStruct((rows, out_width),...  65.7 us
    unnamed x3, local copies, waits for them, and re-layouts  4.32 us

profile of v3, /device:TPU:0, one launch (start us, length us, event | category | flops | bytes accessed | tf_op | source)
XLA Modules:
  0.0 71.4 jit_solution(7146324644034681472)
XLA Ops:
  0.0 1.3 %reshape.3.gain_ref = f32[4,1024]{1,0:T(4,128)} reshape(f32[4096]{0:T(1024)} %param.8) | data formatting | bytes 32768 | tf_op jit(solution)/shard_map/reshape | solution.py:365
  1.3 1.4 %copy.8.ids_ref = s32[64,8]{1,0:T(8,128)} copy(s32[64,8]{0,1:T(8,128)} %param.9) | data formatting | bytes 4096 | tf_op args[2]
  2.7 1.4 %copy.9.gw_ref = f32[64,8]{1,0:T(8,128)} copy(f32[64,8]{0,1:T(8,128)} %param.10) | data formatting | bytes 4096 | tf_op args[3]
  4.1 65.7 %shard_map.73 = bf16[64,1024]{1,0:T(8,128)(2,1)} custom-call(bf16[64,1024]{1,0:T(8,128)(2,1)} %tok_ref.1, f32[4,1024]{1,0:T(4,128)} %reshape.3.gain_ref, s32[64,8]{1,0:T(8,128)} %copy.8.ids_ref, f32[64,8]{1,0:T(8,128)} %copy.9.gw_ref, bf16[16,192,4096]{2,1,0:T(8,128)(2,1)} %gate_ref.1, bf16[16,192,4096]{2,1,0:T(8,128)(2,1)} %up_ref.1, ...), custom_call_target="tpu_custom_call" | custom-call | flops 19327352832 | bytes 75497472 | tf_op jit(solution)/shard_map/pallas_call | solution.py:334
  69.8 1.6 %copy.11 = bf16[64,1024]{1,0:T(8,128)(2,1)} copy(bf16[64,1024]{1,0:T(8,128)(2,1)} %shard_map.73) | data formatting | bytes 262144

commit v4 on v3

--- a/solution.py
+++ b/solution.py
@@ -153,13 +153,14 @@
             src_ref=src, dst_ref=dst, send_sem=ss, recv_sem=rs, device_id=to, device_id_type=MESH
         )
 
-    for e in range(deep_gu):
-        for c in weights(e, e):
-            c.start()
-    for e in range(deep_dn):
-        for c in downs(e, e):
-            c.start()
-
+    ahead = [weights(p, p) for p in range(deep_gu)] + [downs(u, u) for u in range(deep_dn)]
+
+    def prefetch(count):
+        for _ in range(min(count, len(ahead))):
+            for c in ahead.pop(0):
+                c.start()
+
+    prefetch(1)
     barrier = pltpu.get_barrier_semaphore()
     for d in range(1, groups):
         pl.semaphore_signal(barrier, inc=1, device_id={"expert": (z + d) % groups}, device_id_type=MESH)
@@ -185,6 +186,7 @@
     ]
     over[0].start()
     near[0].start()
+    prefetch(1)
 
     lane = lax.broadcasted_iota(jnp.int32, (rows, lanes), 1)
     member = jnp.zeros((rows, lanes), jnp.float32)
@@ -208,29 +210,39 @@
     for c in told:
         c.start()
 
+    step = 32
+
+    def norm(d):
+        near[d].wait_recv()
+        on[d].wait_recv()
+        base = (z + groups - d) % groups * rows
+
+        @pl.loop(0, rows // step)
+        def _(r):
+            at = pl.ds(pl.multiple_of(base + r * step, step), step)
+            values = [raw[s, at, :].astype(jnp.float32) for s in range(shards)]
+            squares = sum(jnp.sum(v * v, axis=1, keepdims=True) for v in values)
+            inv_scale = lax.rsqrt(squares / (shards * width) + epsilon)
+            for s in range(shards):
+                xn[at, s * width : (s + 1) * width] = (values[s] * inv_scale * gain_ref[s : s + 1, :]).astype(
+                    jnp.bfloat16
+                )
+
     for d in range(1, groups):
         first[d - 1].wait_recv()
         over[d].start()
         near[d].start()
+        prefetch(1)
     for d in range(groups):
         over[d].wait_recv()
         on[d].start()
+        prefetch(3)
+        if d > 0:
+            norm(d - 1)
+    prefetch(len(ahead))
+    norm(groups - 1)
     for c in told:
         c.wait_recv()
-    for d in range(groups):
-        near[d].wait_recv()
-        on[d].wait_recv()
-
-    step = 32
-
-    @pl.loop(0, total // step)
-    def _(r):
-        at = pl.ds(pl.multiple_of(r * step, step), step)
-        values = [raw[s, at, :].astype(jnp.float32) for s in range(shards)]
-        squares = sum(jnp.sum(v * v, axis=1, keepdims=True) for v in values)
-        inv_scale = lax.rsqrt(squares / (shards * width) + epsilon)
-        for s in range(shards):
-            xn[at, s * width : (s + 1) * width] = (values[s] * inv_scale * gain_ref[s : s + 1, :]).astype(jnp.bfloat16)
 
     def column(which, e):
         table = info[:, which].reshape(total, lanes)

time: 72.2 us -> 71.2 us (0.986)
  no operation moved by 1% of the time
where the time goes in v4:
time: 71.2 us; the launch traced here: 70.9 us
  Pallas kernels  65.2 us (92%)
  local copies, waits for them, and re-layouts  5.64 us (8%)
    pallas_call x1, Pallas kernels, kernel_form(): pl.pallas_call(kernel, out_shape=jax.ShapeDtypeStruct((rows, out_width),...  65.2 us
    unnamed x3, local copies, waits for them, and re-layouts  4.32 us

profile of v4, /device:TPU:0, one launch (start us, length us, event | category | flops | bytes accessed | tf_op | source)
XLA Modules:
  0.0 70.9 jit_solution(2872062518980770068)
XLA Ops:
  0.0 1.3 %reshape.3.gain_ref = f32[4,1024]{1,0:T(4,128)} reshape(f32[4096]{0:T(1024)} %param.8) | data formatting | bytes 32768 | tf_op jit(solution)/shard_map/reshape | solution.py:377
  1.3 1.4 %copy.8.ids_ref = s32[64,8]{1,0:T(8,128)} copy(s32[64,8]{0,1:T(8,128)} %param.9) | data formatting | bytes 4096 | tf_op args[2]
  2.7 1.4 %copy.9.gw_ref = f32[64,8]{1,0:T(8,128)} copy(f32[64,8]{0,1:T(8,128)} %param.10) | data formatting | bytes 4096 | tf_op args[3]
  4.1 65.2 %shard_map.73 = bf16[64,1024]{1,0:T(8,128)(2,1)} custom-call(bf16[64,1024]{1,0:T(8,128)(2,1)} %tok_ref.1, f32[4,1024]{1,0:T(4,128)} %reshape.3.gain_ref, s32[64,8]{1,0:T(8,128)} %copy.8.ids_ref, f32[64,8]{1,0:T(8,128)} %copy.9.gw_ref, bf16[16,192,4096]{2,1,0:T(8,128)(2,1)} %gate_ref.1, bf16[16,192,4096]{2,1,0:T(8,128)(2,1)} %up_ref.1, ...), custom_call_target="tpu_custom_call" | custom-call | flops 19327352832 | bytes 75497472 | tf_op jit(solution)/shard_map/pallas_call | solution.py:346
  69.3 1.6 %copy.11 = bf16[64,1024]{1,0:T(8,128)(2,1)} copy(bf16[64,1024]{1,0:T(8,128)(2,1)} %shard_map.73) | data formatting | bytes 262144
